TPU v7x, 256 devices: a whole 4x4x8 slice. The times are simulated.
256 devices in a mesh: dp: 16 (over y_lo, x, core), mp: 16 (over y_hi, z).
Axes of the slice: x: 4, y: 4 (y_hi: 2, y_lo: 2; y = y_hi * 2 + y_lo), z: 8, core: 2. Of those that a mesh axis runs over, the one named last changes fastest.
Arguments:
- inputs: bfloat16 [2048, 12288], P('mp', 'dp'), may hold values from -6 to 6
- pre_act: bfloat16 [2048, 36864], P('dp', 'mp'), may hold values from -8 to 8
- out_grad: bfloat16 [2048, 36864], P('dp', 'mp'), may hold values from -1 to 1
- weight: bfloat16 [12288, 36864], P('dp', 'mp'), may hold values from -0.0546875 to 0.0546875
Outputs:
- input_grad: bfloat16 [2048, 12288], P('mp', 'dp')
- weight_grad: float32 [12288, 36864], P('dp', 'mp')
All inputs are finite; a program needn't handle non-finite values.
Results may differ from a plain program's by a relative error of at most 0.0049.
Values may be sent and summed in bfloat16 or wider, within the bound.
A program may use at most 128 MiB of HBM per device.

v0:
```python
import jax
import jax.numpy as jnp
from jax import lax
from jax.sharding import PartitionSpec as P

gelu_scale = 0.7978845608
gelu_cubic = 0.044715


def gelu_slope(values):
    inner = gelu_scale * (values + gelu_cubic * values * values * values)
    tanh_part = jnp.tanh(inner)
    return 0.5 * (1.0 + tanh_part) + 0.5 * values * (1.0 - tanh_part * tanh_part) * gelu_scale * (
        1.0 + 3.0 * gelu_cubic * values * values
    )


def body(inputs, pre_act, out_grad, weight):
    slope = gelu_slope(pre_act.astype(jnp.float32))
    hidden_grad = (out_grad.astype(jnp.float32) * slope).astype(jnp.bfloat16)
    panels = lax.all_gather(inputs, "mp", axis=0, tiled=True)
    shard_piece = lax.all_gather(hidden_grad, "dp", axis=0, tiled=True)
    collected = shard_piece
    tile_part = lax.dot_general(
        shard_piece, weight, (((1,), (1,)), ((), ())), preferred_element_type=jnp.float32
    )
    input_part = tile_part
    collected, input_part = (collected, input_part)
    weight_grad = lax.dot_general(
        panels, collected, (((0,), (0,)), ((), ())), preferred_element_type=jnp.float32
    )
    input_grad = lax.psum_scatter(input_part, "mp", scatter_dimension=0, tiled=True)
    return (input_grad.astype(jnp.bfloat16), weight_grad)


def solution(mesh):
    in_specs = (P("mp", "dp"), P("dp", "mp"), P("dp", "mp"), P("dp", "mp"))
    out_specs = (P("mp", "dp"), P("dp", "mp"))
    return jax.shard_map(body, mesh=mesh, in_specs=in_specs, out_specs=out_specs, check_vma=False)
```

profile of v0, /device:TPU:12, one launch (start us, length us, event | category | flops | bytes accessed | tf_op | source)
XLA Modules:
  0.0 398.0 jit_solution(5672098607494075401)
XLA Ops:
  7.2 0.0 copy-start
  7.2 0.0 all-gather.3.cloned.1.call-start
  7.2 3.0 fusion.7
  10.3 0.0 all-gather.3.cloned.1.call-update
  10.3 0.0 all-gather.5.cloned.1.call-start
  10.3 0.7 all-gather.5.cloned.1.call-update
  11.0 0.0 reduce-scatter.2.cloned.1.call-start
  11.1 61.5 %all-gather.3.cloned.1.call-done = bf16[2048,2304]{1,0:T(8,128)(2,1)} async-done(((bf16[128,2304]{1,0:T(8,128)(2,1)}), bf16[2048,2304]{1,0:T(8,128)(2,1)}) %all-gather.3.cloned.1.call-update) | async-done | bytes 9437200 | tf_op jit(solution)/shard_map/all_gather | solution.py:22
  72.6 0.0 copy-done
  72.6 11.7 %fusion.9 = f32[2048,768]{1,0:T(8,128)} fusion(bf16[2048,2304]{1,0:T(8,128)(2,1)} %all-gather.3.cloned.1.call-done, bf16[768,2304]{1,0:T(8,128)(2,1)S(1)} %copy-done), kind=kOutput, calls=%fused_computation.17 | convolution fusion | flops 7247757312 | bytes 19267584 | tf_op jit(solution)/shard_map/dot_general | solution.py:24
  84.3 0.0 reduce-scatter.2.cloned.1.call-update
  84.4 84.4 %all-gather.5.cloned.1.call-done = bf16[2048,768]{1,0:T(8,128)(2,1)} async-done(((bf16[128,768]{1,0:T(8,128)(2,1)}), bf16[2048,768]{1,0:T(8,128)(2,1)}) %all-gather.5.cloned.1.call-update) | async-done | bytes 3145744 | tf_op jit(solution)/shard_map/all_gather | solution.py:21
  168.8 12.9 %convolution_bitcast_fusion = f32[768,2304]{0,1:T(8,128)} fusion(bf16[2048,2304]{1,0:T(8,128)(2,1)} %all-gather.3.cloned.1.call-done, bf16[2048,768]{1,0:T(8,128)(2,1)} %all-gather.5.cloned.1.call-done), kind=kOutput, calls=%fused_computation | convolution fusion | flops 7247757312 | bytes 19660800 | tf_op jit(solution)/shard_map/dot_general | solution.py:29
  181.7 8.2 %copy.6 = f32[768,2304]{1,0:T(8,128)} copy(f32[768,2304]{0,1:T(8,128)} %convolution_bitcast_fusion) | data formatting | bytes 14155776
  189.9 199.9 %reduce-scatter.2.cloned.1.call-done = f32[128,768]{1,0:T(8,128)} async-done(((f32[2048,768]{1,0:T(8,128)}), f32[128,768]{1,0:T(8,128)}) %reduce-scatter.2.cloned.1.call-update) | async-done | bytes 393232 | tf_op jit(solution)/shard_map/reduce_scatter | solution.py:32
  389.8 1.7 convert_element_type.15
Async XLA Ops:
  7.2 65.4 %copy-start = (bf16[768,2304]{1,0:T(8,128)(2,1)S(1)}, bf16[768,2304]{1,0:T(8,128)(2,1)}, u32[]{:S(2)}) copy-start(bf16[768,2304]{1,0:T(8,128)(2,1)} %param.7) | copy-start | bytes 10616836
  7.2 65.4 %all-gather.3.cloned.1.call-start = ((), (), s32[]{:S(2)}) async-start(), calls=%async_computation.1 | async-start | bytes 10027008 | tf_op jit(solution)/shard_map/all_gather | solution.py:22
  10.3 158.5 %all-gather.5.cloned.1.call-start = ((), (), s32[]{:S(2)}) async-start(), calls=%async_computation.3 | async-start | bytes 3342336 | tf_op jit(solution)/shard_map/all_gather | solution.py:21
  11.0 378.7 %reduce-scatter.2.cloned.1.call-start = ((), (), s32[]{:S(2)}) async-start(), calls=%async_computation.2 | async-start | bytes 6684672 | tf_op jit(solution)/shard_map/reduce_scatter | solution.py:32
Sparse Core Ops, SparseCore 0:
  10.4 62.1 all-gather.2
  75.2 93.5 all-gather.4
  173.0 216.7 reduce-scatter.1
where the time goes:
time: 399 us; the launch traced here: 398 us
  waiting for transfers between devices  347 us (87%)
  matrix products  24.6 us (6%)
  between operations  13.8 us (3%)
  local copies, waits for them, and re-layouts  8.19 us (2%)
  other arithmetic  4.72 us (1%)
    reduce_scatter x1, waiting for transfers between devices, body(): lax.psum_scatter(input_part, 'mp', scatter_dimension=0, tiled=True)  200 us
    all_gather x1, waiting for transfers between devices, body(): panels = lax.all_gather(inputs, 'mp', axis=0, tiled=True)  84.4 us
    all_gather x1, waiting for transfers between devices, body(): shard_piece = lax.all_gather(hidden_grad, 'dp', axis=0, tiled=True)  61.5 us
    dot_general x1, matrix products, body(): lax.dot_general(panels, collected, (((0,), (0,)), ((), ())), preferred_el...  12.9 us
    dot_general x1, matrix products, body(): lax.dot_general(shard_piece, weight, (((1,), (1,)), ((), ())), preferred_...  11.7 us
    unnamed x3, local copies, waits for them, and re-layouts  8.19 us
  transfers between devices with their start and end apart: 3, of which 3 were waited for; matrix products, arithmetic and copies ran while one was open for 8% of the time, Pallas kernels for 0%

commit v1 on v0

v1 whole, which is shorter than its diff:
```python
import jax
import jax.numpy as jnp
from jax import lax
from jax.experimental import pallas as pl
from jax.experimental.pallas import tpu as pltpu
from jax.sharding import PartitionSpec as P

MESH = pl.DeviceIdType.MESH
gelu_scale = 0.7978845608
gelu_cubic = 0.044715

NX, NZ = 4, 8


def gelu_slope(values):
    inner = gelu_scale * (values + gelu_cubic * values * values * values)
    tanh_part = jnp.tanh(inner)
    return 0.5 * (1.0 + tanh_part) + 0.5 * values * (1.0 - tanh_part * tanh_part) * gelu_scale * (
        1.0 + 3.0 * gelu_cubic * values * values
    )


NAMES = {}


def name_all():
    def add(*key):
        NAMES[key] = len(NAMES)

    for k in range(2):
        for kind in ("xp_own", "xm_own", "xp_yl", "xm_yl", "yl"):
            add(kind, k)
    for kind in ("xp_f", "xm_f", "xp_fy", "xm_fy"):
        add(kind)
    for k in range(9):
        add("sb", k)
    add("ya1")
    add("ya2")
    for row in ("own", "other"):
        for s in range(4):
            add("al", row, s)
        for s in range(3):
            add("as", row, s)
    for q in range(8):
        add("ry1", q)
        add("ry2", q)
    for s in range(4):
        add("rl", s)
    for s in range(3):
        add("rs", s)


name_all()


def kernel(
    inputs_hbm, pre_hbm, grad_hbm, weight_hbm, ig_hbm, wg_hbm,
    in_own, pre, grad, weight, hid, acts, acts_pass, kept, sent, passed, received,
    long_out, long_in, short_out, short_in, ig, wg_tile, send_sem, recv_sem, load_sem, store_sem,
):
    tokens = in_own.shape[0]
    feats = in_own.shape[1]
    half = tokens // 2
    pair_tokens = 2 * tokens
    col = 256
    n_cols = pre.shape[1] // col
    f_cols = feats // col

    dp, mp = lax.axis_index("dp"), lax.axis_index("mp")
    c = lax.rem(dp, 2)
    x = lax.rem(dp // 2, NX)
    yl = dp // (2 * NX)
    z = lax.rem(mp, NZ)
    yh = mp // NZ
    y = yh * 2 + yl
    d = 1 - 2 * c

    def xat(off):
        return lax.rem(x + off + NX, NX)

    def zat(off):
        return lax.rem(z + off + NZ, NZ)

    def device(xx, yy, zz, cc):
        return (((lax.rem(yy, 2)) * NX + xx) * 2 + cc, (yy // 2) * NZ + zz)

    def yat(off):
        return lax.rem(y + off + 4, 4)

    other = 1 - yl
    XP = device(xat(1), y, z, c)
    XM = device(xat(-1), y, z, c)
    YL = device(x, yh * 2 + other, z, c)
    SB = device(x, y, z, 1 - c)
    ZL = device(x, y, zat(d), c)
    ZS = device(x, y, zat(-d), c)
    YD = device(x, yat(d), z, c)
    YU = device(x, yat(-d), z, c)

    copies = []

    def make(key, src, dst, to):
        i = NAMES[key]
        return pltpu.make_async_remote_copy(
            src_ref=src, dst_ref=dst, send_sem=send_sem.at[i], recv_sem=recv_sem.at[i],
            device_id=to, device_id_type=MESH,
        )

    def send(key, src, dst, to):
        copy = make(key, src, dst, to)
        copy.start()
        copies.append(copy)

    def arrived(key, dst):
        make(key, dst, dst, XP).wait_recv()

    loads = [
        pltpu.make_async_copy(inputs_hbm, in_own, load_sem.at[0]),
        pltpu.make_async_copy(pre_hbm, pre, load_sem.at[1]),
        pltpu.make_async_copy(grad_hbm, grad, load_sem.at[2]),
        pltpu.make_async_copy(weight_hbm, weight, load_sem.at[3]),
    ]
    for load in loads:
        load.start()

    barrier = pltpu.get_barrier_semaphore()
    for peer in (XP, XM, SB, ZL, ZS, YD, YU):
        pl.semaphore_signal(barrier, inc=1, device_id=peer, device_id_type=MESH)
    pl.semaphore_wait(barrier, 7)

    def act(row, zz):
        at = (row * NZ + zz) * tokens
        return acts.at[:, pl.ds(pl.multiple_of(at, tokens), tokens)]

    loads[0].wait()
    act(yh, z)[...] = in_own[...].T
    send(("al", "own", 0), act(yh, z), act(yh, z), ZL)
    send(("as", "own", 0), act(yh, z), act(yh, z), ZS)
    send(("ya1",), act(yh, z), acts_pass, YD)

    def rows(xx, row, cc, k=None):
        at = ((row * NX + xx) * 2 + cc) * tokens
        if k is None:
            return hid.at[pl.ds(pl.multiple_of(at, tokens), tokens)]
        return hid.at[pl.ds(pl.multiple_of(at + k * half, half), half)]

    loads[1].wait()
    loads[2].wait()
    own = ((yl * NX + x) * 2 + c) * tokens
    for k in range(2):
        @pl.loop(0, half // 16)
        def _(i):
            at = k * half + i * 16
            slope = gelu_slope(pre[pl.ds(at, 16)].astype(jnp.float32))
            value = grad[pl.ds(at, 16)].astype(jnp.float32) * slope
            hid[pl.ds(pl.multiple_of(own + at, 16), 16)] = value.astype(jnp.bfloat16)

        mine = rows(x, yl, c, k)
        send(("yl", k), mine, mine, YL)
        send(("xp_own", k), mine, mine, XP)
        send(("xm_own", k), mine, mine, XM)
        send(("sb", k), mine, mine, SB)

    def sibling(q, xx, row):
        block = rows(xx, row, c)
        send(("sb", q), block, block, SB)

    def have_sibling(q, xx, row):
        if q == 0:
            for k in range(2):
                arrived(("sb", k), rows(xx, row, 1 - c, k))
        else:
            arrived(("sb", q + 1), rows(xx, row, 1 - c))

    def partial(q, xx, row):
        have_sibling(q, xx, row)
        at = pl.multiple_of((row * NX + xx) * pair_tokens, pair_tokens)
        zz = 2 * xx

        @pl.loop(0, f_cols)
        def _(n):
            features = pl.ds(pl.multiple_of(n * col, col), col)
            value = lax.dot_general(
                hid[pl.ds(at, pair_tokens)], weight[features],
                (((1,), (1,)), ((), ())), preferred_element_type=jnp.float32,
            )

            @pl.when(row == yh)
            def _():
                kept[zz, :, features] = value[:tokens]
                kept[zz + 1, :, features] = value[tokens:]

            @pl.when(row != yh)
            def _():
                sent[zz, :, features] = value[:tokens].astype(jnp.bfloat16)
                sent[zz + 1, :, features] = value[tokens:].astype(jnp.bfloat16)

    order = (0, 1, -1, 2)

    def y_send(q):
        for b in range(2):
            at = 2 * xat(order[q]) + b
            make(("ry1", 2 * q + b), sent.at[at], passed.at[at], YD).start()

    def y_pass(q):
        for b in range(2):
            at = 2 * xat(order[q]) + b
            arrived(("ry1", 2 * q + b), passed.at[at])
            make(("ry2", 2 * q + b), passed.at[at], received.at[at], YD).start()

    early_send = yl != yh
    up = yat(-d)
    early_pass = lax.rem(up, 2) != up // 2

    def act_long(row, name, s):
        arrived(("al", name, s), act(row, zat(-d * (s + 1))))
        if s < 3:
            block = act(row, zat(-d * (s + 1)))
            send(("al", name, s + 1), block, block, ZL)

    def act_short(row, name, s):
        arrived(("as", name, s), act(row, zat(d * (s + 1))))
        if s < 2:
            block = act(row, zat(d * (s + 1)))
            send(("as", name, s + 1), block, block, ZS)

    other_row = 1 - yh
    arrived(("ya1",), acts_pass)
    send(("ya2",), acts_pass, act(up // 2, z), YD)

    loads[3].wait()
    partial(0, x, yl)

    @pl.when(early_send)
    def _():
        y_send(0)

    arrived(("ya2",), act(other_row, z))
    send(("al", "other", 0), act(other_row, z), act(other_row, z), ZL)
    send(("as", "other", 0), act(other_row, z), act(other_row, z), ZS)

    for k in range(2):
        block = rows(x, other, c, k)
        arrived(("yl", k), block)
        send(("xp_yl", k), block, block, XP)
        send(("xm_yl", k), block, block, XM)
        if k == 0:
            act_long(yh, "own", 0)
            act_short(yh, "own", 0)
    sibling(5, x, other)

    for k in range(2):
        arrived(("xp_own", k), rows(xat(-1), yl, c, k))
        arrived(("xm_own", k), rows(xat(1), yl, c, k))
        if k == 0:
            block = rows(xat(-1), yl, c, 0)
            send(("xp_f",), block, block, XP)
        else:
            block = rows(xat(1), yl, c, 1)
            send(("xm_f",), block, block, XM)
    sibling(2, xat(1), yl)
    sibling(3, xat(-1), yl)

    partial(4, x, other)

    @pl.when(jnp.logical_not(early_send))
    def _():
        y_send(0)

    act_long(other_row, "other", 0)
    act_short(other_row, "other", 0)

    partial(1, xat(1), yl)

    @pl.when(early_send)
    def _():
        y_send(1)

    act_long(yh, "own", 1)
    act_short(yh, "own", 1)
    partial(2, xat(-1), yl)

    @pl.when(early_send)
    def _():
        y_send(2)

    @pl.when(early_pass)
    def _():
        for q in range(3):
            y_pass(q)

    @pl.when(jnp.logical_not(early_pass))
    def _():
        y_pass(0)

    for k in range(2):
        arrived(("xp_yl", k), rows(xat(-1), other, c, k))
        arrived(("xm_yl", k), rows(xat(1), other, c, k))
        if k == 0:
            block = rows(xat(-1), other, c, 0)
            send(("xp_fy",), block, block, XP)
        else:
            block = rows(xat(1), other, c, 1)
            send(("xm_fy",), block, block, XM)
    sibling(6, xat(1), other)
    sibling(7, xat(-1), other)
    act_long(other_row, "other", 1)
    act_short(other_row, "other", 1)

    arrived(("xp_f",), rows(xat(2), yl, c, 0))
    arrived(("xm_f",), rows(xat(2), yl, c, 1))
    sibling(4, xat(2), yl)
    partial(5, xat(1), other)

    @pl.when(jnp.logical_not(early_send))
    def _():
        y_send(1)

    partial(6, xat(-1), other)

    @pl.when(jnp.logical_not(early_send))
    def _():
        y_send(2)

    act_long(yh, "own", 2)
    act_short(yh, "own", 2)
    partial(3, xat(2), yl)

    @pl.when(early_send)
    def _():
        y_send(3)

    @pl.when(early_pass)
    def _():
        y_pass(3)

    @pl.when(jnp.logical_not(early_pass))
    def _():
        y_pass(1)
        y_pass(2)

    arrived(("xp_fy",), rows(xat(2), other, c, 0))
    arrived(("xm_fy",), rows(xat(2), other, c, 1))
    sibling(8, xat(2), other)
    act_long(other_row, "other", 2)
    act_short(other_row, "other", 2)
    partial(7, xat(2), other)

    @pl.when(jnp.logical_not(early_send))
    def _():
        y_send(3)

    @pl.when(jnp.logical_not(early_pass))
    def _():
        y_pass(3)

    act_long(yh, "own", 3)
    act_long(other_row, "other", 3)

    for q in range(4):
        for b in range(2):
            arrived(("ry2", 2 * q + b), received.at[2 * xat(order[q]) + b])

    def share(at):
        return kept[at] + received[at].astype(jnp.float32)

    def tiles(first, last):
        @pl.loop(first, last)
        def _(n):
            columns = pl.ds(pl.multiple_of(n * col, col), col)
            wg_tile[:, columns] = jnp.dot(acts[...], hid[:, columns], preferred_element_type=jnp.float32)
            pltpu.make_async_copy(wg_tile.at[:, columns], wg_hbm.at[:, columns], store_sem.at[n]).start()

    cuts = (0, 2, 4, 6, 8)
    for s in range(4):
        total = share(zat(d * (4 - s)))
        if s > 0:
            arrived(("rl", s - 1), long_in.at[s - 1])
            total = total + long_in[s - 1].astype(jnp.float32)
        long_out[s] = total.astype(jnp.bfloat16)
        send(("rl", s), long_out.at[s], long_in.at[s], ZL)
        if s < 3:
            total = share(zat(-d * (3 - s)))
            if s > 0:
                arrived(("rs", s - 1), short_in.at[s - 1])
                total = total + short_in[s - 1].astype(jnp.float32)
            short_out[s] = total.astype(jnp.bfloat16)
            send(("rs", s), short_out.at[s], short_in.at[s], ZS)
        tiles(cuts[s], cuts[s + 1])
    tiles(cuts[4], n_cols)

    total = share(z)
    arrived(("rs", 2), short_in.at[2])
    total = total + short_in[2].astype(jnp.float32)
    arrived(("rl", 3), long_in.at[3])
    total = total + long_in[3].astype(jnp.float32)
    ig[...] = total.astype(jnp.bfloat16)
    last = pltpu.make_async_copy(ig, ig_hbm, load_sem.at[0])
    last.start()

    for copy in copies:
        copy.wait_send()
    for q in range(4):
        for b in range(2):
            at = 2 * xat(order[q]) + b
            make(("ry1", 2 * q + b), sent.at[at], passed.at[at], YD).wait_send()
            make(("ry2", 2 * q + b), passed.at[at], received.at[at], YD).wait_send()
    for n in range(n_cols):
        columns = pl.ds(n * col, col)
        pltpu.make_async_copy(wg_tile.at[:, columns], wg_hbm.at[:, columns], store_sem.at[n]).wait()
    last.wait()


def body(inputs, pre_act, out_grad, weight):
    tokens, feats = inputs.shape
    hidden = pre_act.shape[1]
    all_tokens = tokens * lax.axis_size("mp")
    bf16, f32 = jnp.bfloat16, jnp.float32
    anywhere = pl.BlockSpec(memory_space=pl.ANY)
    return tuple(
        pl.pallas_call(
            kernel,
            out_shape=(
                jax.ShapeDtypeStruct((tokens, feats), bf16),
                jax.ShapeDtypeStruct((feats, hidden), f32),
            ),
            in_specs=[anywhere] * 4,
            out_specs=(anywhere, anywhere),
            scratch_shapes=[
                pltpu.VMEM((tokens, feats), bf16),
                pltpu.VMEM((tokens, hidden), bf16),
                pltpu.VMEM((tokens, hidden), bf16),
                pltpu.VMEM((feats, hidden), bf16),
                pltpu.VMEM((all_tokens, hidden), bf16),
                pltpu.VMEM((feats, all_tokens), bf16),
                pltpu.VMEM((feats, tokens), bf16),
                pltpu.VMEM((NZ, tokens, feats), f32),
                pltpu.VMEM((NZ, tokens, feats), bf16),
                pltpu.VMEM((NZ, tokens, feats), bf16),
                pltpu.VMEM((NZ, tokens, feats), bf16),
                pltpu.VMEM((4, tokens, feats), bf16),
                pltpu.VMEM((4, tokens, feats), bf16),
                pltpu.VMEM((3, tokens, feats), bf16),
                pltpu.VMEM((3, tokens, feats), bf16),
                pltpu.VMEM((tokens, feats), bf16),
                pltpu.VMEM((feats, hidden), f32),
                pltpu.SemaphoreType.DMA((len(NAMES),)),
                pltpu.SemaphoreType.DMA((len(NAMES),)),
                pltpu.SemaphoreType.DMA((4,)),
                pltpu.SemaphoreType.DMA((hidden // 256,)),
            ],
            compiler_params=pltpu.CompilerParams(
                collective_id=0, has_side_effects=True, vmem_limit_bytes=56 * 2**20
            ),
            cost_estimate=pl.CostEstimate(
                flops=4 * all_tokens * feats * hidden, bytes_accessed=12 * 2**20,
                transcendentals=tokens * hidden,
            ),
            name="ffn_input_backward",
        )(inputs, pre_act, out_grad, weight)
    )


def solution(mesh):
    in_specs = (P("mp", "dp"), P("dp", "mp"), P("dp", "mp"), P("dp", "mp"))
    out_specs = (P("mp", "dp"), P("dp", "mp"))
    return jax.shard_map(body, mesh=mesh, in_specs=in_specs, out_specs=out_specs, check_vma=False)
```

time: 399 us -> 109 us (0.27)
  the two profiles are of different devices: /device:TPU:12 before, /device:TPU:16 now
where the time goes in v1:
time: 109 us; the launch traced here: 108 us
  Pallas kernels  99.8 us (92%)
  local copies, waits for them, and re-layouts  8.04 us (7%)
    pallas_call x1, Pallas kernels, body(): pl.pallas_call(kernel, out_shape=(jax.ShapeDtypeStruct((tokens, feats), b...  99.8 us
    unnamed x2, local copies, waits for them, and re-layouts  8.04 us

profile of v1, /device:TPU:16, one launch (start us, length us, event | category | flops | bytes accessed | tf_op | source)
XLA Modules:
  0.0 108.5 jit_solution(8422853999860807542)
XLA Ops:
  0.6 99.8 %ffn_input_backward.1 = (bf16[128,768]{1,0:T(8,128)(2,1)}, f32[768,2304]{1,0:T(8,128)}) custom-call(bf16[128,768]{1,0:T(8,128)(2,1)} %inputs_hbm.1, bf16[128,2304]{1,0:T(8,128)(2,1)} %pre_hbm.1, bf16[128,2304]{1,0:T(8,128)(2,1)} %grad_hbm.1, bf16[768,2304]{1,0:T(8,128)(2,1)} %weight_hbm.1), custom_call_target="tpu_custom_call" | custom-call | flops 14495514624 | bytes 12582912 | tf_op jit(solution)/shard_map/ffn_input_backward/pallas_call | solution.py:421
  100.4 1.6 %copy.8 = bf16[128,768]{1,0:T(8,128)(2,1)} copy(bf16[128,768]{1,0:T(8,128)(2,1)} %get-tuple-element.4) | data formatting | bytes 393216
  102.0 6.4 %copy.9 = f32[768,2304]{1,0:T(8,128)} copy(f32[768,2304]{1,0:T(8,128)} %get-tuple-element.5) | data formatting | bytes 14155776

commit v2 on v0

v2 whole, which is shorter than its diff:
```python
import jax
import jax.numpy as jnp
from jax import lax
from jax.experimental import pallas as pl
from jax.experimental.pallas import tpu as pltpu
from jax.sharding import PartitionSpec as P

MESH = pl.DeviceIdType.MESH
gelu_scale = 0.7978845608
gelu_cubic = 0.044715

NX, NZ = 4, 8


def gelu_slope(values):
    inner = gelu_scale * (values + gelu_cubic * values * values * values)
    tanh_part = jnp.tanh(inner)
    return 0.5 * (1.0 + tanh_part) + 0.5 * values * (1.0 - tanh_part * tanh_part) * gelu_scale * (
        1.0 + 3.0 * gelu_cubic * values * values
    )


NAMES = {}


def name_all():
    def add(*key):
        NAMES[key] = len(NAMES)

    for k in range(2):
        for kind in ("xp_own", "xm_own", "xp_yl", "xm_yl", "yl"):
            add(kind, k)
    for kind in ("xp_f", "xm_f", "xp_fy", "xm_fy"):
        add(kind)
    for q in range(8):
        add("sb", q)
    add("ya")
    for row in ("own", "other"):
        for s in range(4):
            add("al", row, s)
        for s in range(3):
            add("as", row, s)
    for q in range(8):
        add("ry", q)
    for q in range(32):
        add("rz", q)


name_all()


def kernel(
    inputs_hbm, pre_hbm, grad_hbm, weight_hbm, ig_hbm, wg_hbm,
    in_own, pre, grad, weight, hid, acts, kept, sent, received, z_out, z_in, ig, wg_tile,
    send_sem, recv_sem, load_sem, store_sem,
):
    tokens = in_own.shape[0]
    feats = in_own.shape[1]
    half = tokens // 2
    pair_tokens = 2 * tokens
    col = 256
    n_cols = pre.shape[1] // col
    f_cols = feats // col

    dp, mp = lax.axis_index("dp"), lax.axis_index("mp")
    c = lax.rem(dp, 2)
    x = lax.rem(dp // 2, NX)
    yl = dp // (2 * NX)
    z = lax.rem(mp, NZ)
    yh = mp // NZ
    d = 1 - 2 * c
    other = 1 - yl
    other_row = 1 - yh

    def xat(off):
        return lax.rem(x + off + NX, NX)

    def zat(off):
        return lax.rem(z + off + NZ, NZ)

    def device(xx, lo, hi, zz, cc):
        return ((lo * NX + xx) * 2 + cc, hi * NZ + zz)

    XP = device(xat(1), yl, yh, z, c)
    XM = device(xat(-1), yl, yh, z, c)
    YL = device(x, other, yh, z, c)
    YH = device(x, yl, other_row, z, c)
    SB = device(x, yl, yh, z, 1 - c)
    ZL = device(x, yl, yh, zat(d), c)
    ZS = device(x, yl, yh, zat(-d), c)

    copies = []

    def make(key, src, dst, to, extra=0):
        i = NAMES[key] + extra
        return pltpu.make_async_remote_copy(
            src_ref=src, dst_ref=dst, send_sem=send_sem.at[i], recv_sem=recv_sem.at[i],
            device_id=to, device_id_type=MESH,
        )

    def send(key, src, to):
        copy = make(key, src, src, to)
        copy.start()
        copies.append(copy)

    def arrived(key, dst, extra=0):
        make(key, dst, dst, XP, extra).wait_recv()

    loads = [
        pltpu.make_async_copy(inputs_hbm, in_own, load_sem.at[0]),
        pltpu.make_async_copy(pre_hbm, pre, load_sem.at[1]),
        pltpu.make_async_copy(grad_hbm, grad, load_sem.at[2]),
        pltpu.make_async_copy(weight_hbm, weight, load_sem.at[3]),
    ]
    for load in loads:
        load.start()

    barrier = pltpu.get_barrier_semaphore()
    for peer in (XP, XM, YL, YH, SB, ZL, ZS):
        pl.semaphore_signal(barrier, inc=1, device_id=peer, device_id_type=MESH)

    def act(row, zz):
        at = (row * NZ + zz) * tokens
        return acts.at[:, pl.ds(pl.multiple_of(at, tokens), tokens)]

    def rows(xx, row, cc, k=None):
        at = ((row * NX + xx) * 2 + cc) * tokens
        if k is None:
            return hid.at[pl.ds(pl.multiple_of(at, tokens), tokens)]
        return hid.at[pl.ds(pl.multiple_of(at + k * half, half), half)]

    def slope_part(k):
        own = ((yl * NX + x) * 2 + c) * tokens

        @pl.loop(0, half // 16)
        def _(i):
            at = k * half + i * 16
            slope = gelu_slope(pre[pl.ds(at, 16)].astype(jnp.float32))
            value = grad[pl.ds(at, 16)].astype(jnp.float32) * slope
            hid[pl.ds(pl.multiple_of(own + at, 16), 16)] = value.astype(jnp.bfloat16)

    def send_part(k):
        mine = rows(x, yl, c, k)
        send(("yl", k), mine, YL)
        send(("xp_own", k), mine, XP)
        send(("xm_own", k), mine, XM)

    loads[1].wait()
    loads[2].wait()
    slope_part(0)
    pl.semaphore_wait(barrier, 7)
    send_part(0)
    loads[0].wait()
    act(yh, z)[...] = in_own[...].T
    send(("al", "own", 0), act(yh, z), ZL)
    send(("as", "own", 0), act(yh, z), ZS)
    send(("ya",), act(yh, z), YH)
    slope_part(1)
    send_part(1)
    send(("sb", 0), rows(x, yl, c), SB)

    order = (0, 1, -1, 2)

    def sibling(q):
        send(("sb", q), rows(xat(order[q % 4]), yl if q < 4 else other, c), SB)

    def partial(q, row):
        xx = xat(order[q])
        arrived(("sb", 0), rows(xx, row, 1 - c), extra=lax.rem(row + yl, 2) * 4 + q)
        at = pl.multiple_of((row * NX + xx) * pair_tokens, pair_tokens)
        zz = 2 * xx

        @pl.loop(0, f_cols)
        def _(n):
            features = pl.ds(pl.multiple_of(n * col, col), col)
            value = lax.dot_general(
                hid[pl.ds(at, pair_tokens)], weight[features],
                (((1,), (1,)), ((), ())), preferred_element_type=jnp.float32,
            )

            @pl.when(row == yh)
            def _():
                kept[zz, :, features] = value[:tokens]
                kept[zz + 1, :, features] = value[tokens:]

            @pl.when(row != yh)
            def _():
                sent[zz, :, features] = value[:tokens].astype(jnp.bfloat16)
                sent[zz + 1, :, features] = value[tokens:].astype(jnp.bfloat16)

    def y_copy(q, b):
        at = 2 * xat(order[q]) + b
        return make(("ry", 2 * q + b), sent.at[at], received.at[at], YH)

    def y_send(q, row):
        @pl.when(row != yh)
        def _():
            for b in range(2):
                y_copy(q, b).start()

    def act_long(name, s):
        block = act(yh if name == "own" else other_row, zat(-d * (s + 1)))
        arrived(("al", name, s), block)
        if s < 3:
            send(("al", name, s + 1), block, ZL)

    def act_short(name, s):
        block = act(yh if name == "own" else other_row, zat(d * (s + 1)))
        arrived(("as", name, s), block)
        if s < 2:
            send(("as", name, s + 1), block, ZS)

    def act_step(name, s):
        act_long(name, s)
        if s < 3:
            act_short(name, s)

    def act_other():
        block = act(other_row, z)
        arrived(("ya",), block)
        send(("al", "other", 0), block, ZL)
        send(("as", "other", 0), block, ZS)

    def z_place(q, b):
        at = 2 * xat(order[q]) + b
        return at, lax.rem((at - z) * d + NZ, NZ)

    def part(h):
        return pl.ds(h * half, half)

    def z_copy(q, b, h):
        at, k = z_place(q, b)
        short = k // 5
        to = device(x, yl, yh, zat(d * (1 - 2 * short)), c)
        return make(
            ("rz", 4 * q + 2 * b + h), z_out.at[at, part(h)], z_in.at[short, at, part(h)], to, extra=16 * short
        )

    def z_arrived(q, b, h, short):
        at, _ = z_place(q, b)
        arrived(("rz", 4 * q + 2 * b + h), z_in.at[short, at, part(h)], extra=16 * short)
        return z_in[short, at, part(h)].astype(jnp.float32)

    def z_step(q, s):
        for b in range(2):
            at, k = z_place(q, b)
            if s < 4:
                here = (k == 5 - s) | (k == 4 + s)
            elif s == 4:
                here = k == 1
            else:
                here = k == 0

            @pl.when(here)
            def _():
                arrived(("ry", 2 * q + b), received.at[at])
                for h in range(2):
                    total = kept[at, part(h)] + received[at, part(h)].astype(jnp.float32)
                    if 1 < s < 5:
                        total = total + z_arrived(q, b, h, k // 5)
                    if s < 5:
                        z_out[at, part(h)] = total.astype(jnp.bfloat16)
                        z_copy(q, b, h).start()
                    else:
                        total = total + z_arrived(q, b, h, 1)
                        total = total + z_arrived(q, b, h, 0)
                        ig[part(h)] = total.astype(jnp.bfloat16)
                if s == 5:
                    pltpu.make_async_copy(ig, ig_hbm, load_sem.at[0]).start()

    def tiles(first, last):
        @pl.loop(first, last)
        def _(n):
            columns = pl.ds(pl.multiple_of(n * col, col), col)
            wg_tile[:, columns] = jnp.dot(acts[...], hid[:, columns], preferred_element_type=jnp.float32)
            pltpu.make_async_copy(wg_tile.at[:, columns], wg_hbm.at[:, columns], store_sem.at[n]).start()

    act_step("own", 0)
    loads[3].wait()
    partial(0, yl)
    y_send(0, yl)
    act_other()
    act_step("own", 1)

    for k in range(2):
        block = rows(x, other, c, k)
        arrived(("yl", k), block)
        send(("xp_yl", k), block, XP)
        send(("xm_yl", k), block, XM)
    sibling(4)
    for k in range(2):
        arrived(("xp_own", k), rows(xat(-1), yl, c, k))
        arrived(("xm_own", k), rows(xat(1), yl, c, k))
    sibling(1)
    sibling(2)
    act_step("other", 0)

    send(("xp_f",), rows(xat(-1), yl, c, 0), XP)
    send(("xm_f",), rows(xat(1), yl, c, 1), XM)
    partial(1, yl)
    y_send(1, yl)
    partial(2, yl)
    y_send(2, yl)
    partial(0, other)
    y_send(0, other)
    act_step("own", 2)
    act_step("other", 1)

    arrived(("xp_f",), rows(xat(2), yl, c, 0))
    arrived(("xm_f",), rows(xat(2), yl, c, 1))
    sibling(3)
    for k in range(2):
        arrived(("xp_yl", k), rows(xat(-1), other, c, k))
        arrived(("xm_yl", k), rows(xat(1), other, c, k))
        if k == 0:
            send(("xp_fy",), rows(xat(-1), other, c, 0), XP)
        else:
            send(("xm_fy",), rows(xat(1), other, c, 1), XM)
    sibling(5)
    sibling(6)
    partial(3, yl)
    y_send(3, yl)
    act_step("own", 3)
    act_step("other", 2)
    partial(1, other)
    y_send(1, other)
    partial(2, other)
    y_send(2, other)

    act_step("other", 3)
    z_step(0, 1)
    z_step(0, 2)
    z_step(1, 1)
    z_step(2, 1)
    z_step(0, 3)
    arrived(("xp_fy",), rows(xat(2), other, c, 0))
    arrived(("xm_fy",), rows(xat(2), other, c, 1))
    sibling(7)
    z_step(1, 2)
    z_step(2, 2)

    partial(3, other)
    y_send(3, other)
    z_step(0, 4)
    z_step(1, 3)
    z_step(2, 3)
    tiles(0, 2)
    z_step(0, 5)
    z_step(1, 4)
    z_step(2, 4)
    tiles(2, 4)
    z_step(3, 1)
    tiles(4, 5)
    z_step(3, 2)
    tiles(5, 6)
    z_step(1, 5)
    z_step(2, 5)
    z_step(3, 3)
    tiles(6, 7)
    z_step(3, 4)
    tiles(7, n_cols)
    z_step(3, 5)

    for copy in copies:
        copy.wait_send()
    for q in range(4):
        for b in range(2):
            y_copy(q, b).wait_send()
            _, k = z_place(q, b)

            @pl.when(k != 0)
            def _():
                for h in range(2):
                    z_copy(q, b, h).wait_send()

    for n in range(n_cols):
        columns = pl.ds(n * col, col)
        pltpu.make_async_copy(wg_tile.at[:, columns], wg_hbm.at[:, columns], store_sem.at[n]).wait()
    pltpu.make_async_copy(ig, ig_hbm, load_sem.at[0]).wait()


def body(inputs, pre_act, out_grad, weight):
    tokens, feats = inputs.shape
    hidden = pre_act.shape[1]
    all_tokens = tokens * lax.axis_size("mp")
    bf16, f32 = jnp.bfloat16, jnp.float32
    anywhere = pl.BlockSpec(memory_space=pl.ANY)
    return tuple(
        pl.pallas_call(
            kernel,
            out_shape=(
                jax.ShapeDtypeStruct((tokens, feats), bf16),
                jax.ShapeDtypeStruct((feats, hidden), f32),
            ),
            in_specs=[anywhere] * 4,
            out_specs=(anywhere, anywhere),
            scratch_shapes=[
                pltpu.VMEM((tokens, feats), bf16),
                pltpu.VMEM((tokens, hidden), bf16),
                pltpu.VMEM((tokens, hidden), bf16),
                pltpu.VMEM((feats, hidden), bf16),
                pltpu.VMEM((all_tokens, hidden), bf16),
                pltpu.VMEM((feats, all_tokens), bf16),
                pltpu.VMEM((NZ, tokens, feats), f32),
                pltpu.VMEM((NZ, tokens, feats), bf16),
                pltpu.VMEM((NZ, tokens, feats), bf16),
                pltpu.VMEM((NZ, tokens, feats), bf16),
                pltpu.VMEM((2, NZ, tokens, feats), bf16),
                pltpu.VMEM((tokens, feats), bf16),
                pltpu.VMEM((feats, hidden), f32),
                pltpu.SemaphoreType.DMA((len(NAMES),)),
                pltpu.SemaphoreType.DMA((len(NAMES),)),
                pltpu.SemaphoreType.DMA((4,)),
                pltpu.SemaphoreType.DMA((hidden // 256,)),
            ],
            compiler_params=pltpu.CompilerParams(
                collective_id=0, has_side_effects=True, vmem_limit_bytes=42 * 2**20
            ),
            cost_estimate=pl.CostEstimate(
                flops=4 * all_tokens * feats * hidden, bytes_accessed=12 * 2**20,
                transcendentals=tokens * hidden,
            ),
            name="ffn_input_backward",
        )(*(pltpu.with_memory_space_constraint(a, pltpu.HBM) for a in (inputs, pre_act, out_grad, weight)))
    )


def solution(mesh):
    in_specs = (P("mp", "dp"), P("dp", "mp"), P("dp", "mp"), P("dp", "mp"))
    out_specs = (P("mp", "dp"), P("dp", "mp"))
    return jax.shard_map(body, mesh=mesh, in_specs=in_specs, out_specs=out_specs, check_vma=False)
```

time: 399 us -> 101 us (0.25)
  waiting for transfers between devices: 347 us -> 0 us
  Pallas kernels: 0 us -> 95.9 us
  matrix products: 24.6 us -> 0 us
  between operations: 13.8 us -> 0.64 us
  other arithmetic: 4.72 us -> 0 us
  local copies, waits for them, and re-layouts: 8.19 us -> 3.64 us
    reduce_scatter x1 -> x0, waiting for transfers between devices: 200 us -> none  [body(): lax.psum_scatter(input_part, 'mp', scatter_dimension=0, tiled=True)]
    all_gather x2 -> x0, waiting for transfers between devices: 146 us -> none  [the longest x1 84.4 us: body(): panels = lax.all_gather(inputs, 'mp', axis=0, tiled=True)]
    pallas_call x0 -> x1, Pallas kernels: none -> 95.9 us  [body(): pl.pallas_call(kernel, out_shape=(jax.ShapeDtypeStruct((tokens, feats), b...]
    dot_general x2 -> x0, matrix products: 24.6 us -> none  [the longest x1 12.9 us: body(): lax.dot_general(panels, collected, (((0,), (0,)), ((), ())), preferred_el...]
    convert_element_type x2 -> x0, other arithmetic: 4.72 us -> none  [the longest x1 3.03 us: body(): hidden_grad = (out_grad.astype(jnp.float32) * slope).astype(jnp.bfloat16)]
    unnamed x3 -> x2, local copies, waits for them, and re-layouts: 8.19 us -> 3.64 us
  transfers between devices with their start and end apart: 3 -> 0, of which waited for: 3 -> 0; matrix products, arithmetic and copies ran while one was open for 8% -> 0% of each run, Pallas kernels for 0% -> 0%
where the time goes in v2:
time: 101 us; the launch traced here: 100 us
  Pallas kernels  95.9 us (95%)
  local copies, waits for them, and re-layouts  3.64 us (4%)
    pallas_call x1, Pallas kernels, body(): pl.pallas_call(kernel, out_shape=(jax.ShapeDtypeStruct((tokens, feats), b...  95.9 us
    unnamed x2, local copies, waits for them, and re-layouts  3.64 us

profile of v2, /device:TPU:12, one launch (start us, length us, event | category | flops | bytes accessed | tf_op | source)
XLA Modules:
  0.0 100.2 jit_solution(16299676344988229929)
XLA Ops:
  0.6 95.9 %ffn_input_backward.1 = (bf16[128,768]{1,0:T(8,128)(2,1)S(1)}, f32[768,2304]{1,0:T(8,128)S(1)}) custom-call(bf16[128,768]{1,0:T(8,128)(2,1)} %inputs_hbm.1, bf16[128,2304]{1,0:T(8,128)(2,1)} %pre_hbm.1, bf16[128,2304]{1,0:T(8,128)(2,1)} %grad_hbm.1, bf16[768,2304]{1,0:T(8,128)(2,1)} %weight_hbm.1), custom_call_target="tpu_custom_call" | custom-call | flops 14495514624 | bytes 12582912 | tf_op jit(solution)/shard_map/ffn_input_backward/pallas_call | solution.py:389
  96.5 0.7 copy.8
  97.2 3.0 %copy.9 = f32[768,2304]{1,0:T(8,128)} copy(f32[768,2304]{1,0:T(8,128)S(1)} %get-tuple-element.5) | data formatting | bytes 14155776

commit v3 on v2

--- a/solution.py
+++ b/solution.py
@@ -10,6 +10,7 @@
 gelu_cubic = 0.044715
 
 NX, NZ = 4, 8
+Z_FIRST = (0, 1, 2, 3)
 
 
 def gelu_slope(values):
@@ -34,15 +35,15 @@
         add(kind)
     for q in range(8):
         add("sb", q)
-    add("ya")
-    for row in ("own", "other"):
-        for s in range(4):
-            add("al", row, s)
-        for s in range(3):
-            add("as", row, s)
+    for s in range(4):
+        add("al", s)
+    for s in range(3):
+        add("as", s)
+    for i in range(8):
+        add("ay", i)
     for q in range(8):
         add("ry", q)
-    for q in range(32):
+    for q in range(64):
         add("rz", q)
 
 
@@ -51,7 +52,7 @@
 
 def kernel(
     inputs_hbm, pre_hbm, grad_hbm, weight_hbm, ig_hbm, wg_hbm,
-    in_own, pre, grad, weight, hid, acts, kept, sent, received, z_out, z_in, ig, wg_tile,
+    in_own, pre, grad, weight, hid, acts, kept, sent, received, z_out, z_in, own_sum, ig, wg_tile,
     send_sem, recv_sem, load_sem, store_sem,
 ):
     tokens = in_own.shape[0]
@@ -152,9 +153,8 @@
     send_part(0)
     loads[0].wait()
     act(yh, z)[...] = in_own[...].T
-    send(("al", "own", 0), act(yh, z), ZL)
-    send(("as", "own", 0), act(yh, z), ZS)
-    send(("ya",), act(yh, z), YH)
+    send(("al", 0), act(yh, z), ZL)
+    send(("as", 0), act(yh, z), ZS)
     slope_part(1)
     send_part(1)
     send(("sb", 0), rows(x, yl, c), SB)
@@ -178,19 +178,24 @@
                 (((1,), (1,)), ((), ())), preferred_element_type=jnp.float32,
             )
 
-            @pl.when(row == yh)
-            def _():
-                kept[zz, :, features] = value[:tokens]
-                kept[zz + 1, :, features] = value[tokens:]
-
-            @pl.when(row != yh)
-            def _():
-                sent[zz, :, features] = value[:tokens].astype(jnp.bfloat16)
-                sent[zz + 1, :, features] = value[tokens:].astype(jnp.bfloat16)
+            def keep():
+                kept[row * NZ + zz, :, features] = value[:tokens]
+                kept[row * NZ + zz + 1, :, features] = value[tokens:]
+
+            if q in Z_FIRST:
+                keep()
+            else:
+                pl.when(row == yh)(keep)
+
+                @pl.when(row != yh)
+                def _():
+                    sent[zz, :, features] = value[:tokens].astype(jnp.bfloat16)
+                    sent[zz + 1, :, features] = value[tokens:].astype(jnp.bfloat16)
 
     def y_copy(q, b):
         at = 2 * xat(order[q]) + b
-        return make(("ry", 2 * q + b), sent.at[at], received.at[at], YH)
+        source = z_out.at[other_row * NZ + at] if q in Z_FIRST else sent.at[at]
+        return make(("ry", 2 * q + b), source, received.at[at], YH)
 
     def y_send(q, row):
         @pl.when(row != yh)
@@ -198,28 +203,25 @@
             for b in range(2):
                 y_copy(q, b).start()
 
-    def act_long(name, s):
-        block = act(yh if name == "own" else other_row, zat(-d * (s + 1)))
-        arrived(("al", name, s), block)
+    def act_step(s):
+        block = act(yh, zat(-d * (s + 1)))
+        arrived(("al", s), block)
         if s < 3:
-            send(("al", name, s + 1), block, ZL)
-
-    def act_short(name, s):
-        block = act(yh if name == "own" else other_row, zat(d * (s + 1)))
-        arrived(("as", name, s), block)
+            send(("al", s + 1), block, ZL)
+            block = act(yh, zat(d * (s + 1)))
+            arrived(("as", s), block)
         if s < 2:
-            send(("as", name, s + 1), block, ZS)
-
-    def act_step(name, s):
-        act_long(name, s)
-        if s < 3:
-            act_short(name, s)
-
-    def act_other():
-        block = act(other_row, z)
-        arrived(("ya",), block)
-        send(("al", "other", 0), block, ZL)
-        send(("as", "other", 0), block, ZS)
+            send(("as", s + 1), block, ZS)
+
+    def act_partner(i, row):
+        return act(row, zat(-d * i if i < 5 else d * (i - 4)))
+
+    def act_send(i):
+        send(("ay", i), act_partner(i, yh), YH)
+
+    def acts_arrived():
+        for i in range(8):
+            arrived(("ay", i), act_partner(i, other_row))
 
     def z_place(q, b):
         at = 2 * xat(order[q]) + b
@@ -228,20 +230,23 @@
     def part(h):
         return pl.ds(h * half, half)
 
-    def z_copy(q, b, h):
-        at, k = z_place(q, b)
-        short = k // 5
-        to = device(x, yl, yh, zat(d * (1 - 2 * short)), c)
-        return make(
-            ("rz", 4 * q + 2 * b + h), z_out.at[at, part(h)], z_in.at[short, at, part(h)], to, extra=16 * short
-        )
-
-    def z_arrived(q, b, h, short):
+    def z_refs(q, b, h, row, short):
         at, _ = z_place(q, b)
-        arrived(("rz", 4 * q + 2 * b + h), z_in.at[short, at, part(h)], extra=16 * short)
-        return z_in[short, at, part(h)].astype(jnp.float32)
-
-    def z_step(q, s):
+        away = lax.rem(row + yh, 2)
+        extra = 32 * away + 16 * short
+        return ("rz", 4 * q + 2 * b + h), z_out.at[row * NZ + at, part(h)], z_in.at[short, row * NZ + at, part(h)], extra
+
+    def z_copy(q, b, h, row):
+        short = z_place(q, b)[1] // 5
+        key, source, target, extra = z_refs(q, b, h, row, short)
+        return make(key, source, target, device(x, yl, yh, zat(d * (1 - 2 * short)), c), extra)
+
+    def z_arrived(q, b, h, row, short):
+        key, _, target, extra = z_refs(q, b, h, row, short)
+        arrived(key, target, extra)
+        return target[...].astype(jnp.float32)
+
+    def z_step(q, s, row):
         for b in range(2):
             at, k = z_place(q, b)
             if s < 4:
@@ -253,35 +258,70 @@
 
             @pl.when(here)
             def _():
+                if q not in Z_FIRST:
+                    arrived(("ry", 2 * q + b), received.at[at])
+                for h in range(2):
+                    total = kept[row * NZ + at, part(h)]
+                    if q not in Z_FIRST:
+                        total = total + received[at, part(h)].astype(jnp.float32)
+                    if 1 < s < 5:
+                        total = total + z_arrived(q, b, h, row, k // 5)
+                    if s < 5:
+                        z_out[row * NZ + at, part(h)] = total.astype(jnp.bfloat16)
+                        z_copy(q, b, h, row).start()
+                        continue
+                    total = total + z_arrived(q, b, h, row, 1)
+                    total = total + z_arrived(q, b, h, row, 0)
+                    if q not in Z_FIRST:
+                        ig[part(h)] = total.astype(jnp.bfloat16)
+                        continue
+
+                    @pl.when(row == yh)
+                    def _():
+                        own_sum[part(h)] = total
+
+                    @pl.when(row != yh)
+                    def _():
+                        z_out[row * NZ + at, part(h)] = total.astype(jnp.bfloat16)
+
+                if s == 5:
+                    if q not in Z_FIRST:
+                        pltpu.make_async_copy(ig, ig_hbm, load_sem.at[0]).start()
+                    else:
+                        @pl.when(row != yh)
+                        def _():
+                            y_copy(q, b).start()
+
+    def finish(q):
+        for b in range(2):
+            at, k = z_place(q, b)
+
+            @pl.when(k == 0)
+            def _():
                 arrived(("ry", 2 * q + b), received.at[at])
-                for h in range(2):
-                    total = kept[at, part(h)] + received[at, part(h)].astype(jnp.float32)
-                    if 1 < s < 5:
-                        total = total + z_arrived(q, b, h, k // 5)
-                    if s < 5:
-                        z_out[at, part(h)] = total.astype(jnp.bfloat16)
-                        z_copy(q, b, h).start()
-                    else:
-                        total = total + z_arrived(q, b, h, 1)
-                        total = total + z_arrived(q, b, h, 0)
-                        ig[part(h)] = total.astype(jnp.bfloat16)
-                if s == 5:
-                    pltpu.make_async_copy(ig, ig_hbm, load_sem.at[0]).start()
+                ig[...] = (own_sum[...] + received[at].astype(jnp.float32)).astype(jnp.bfloat16)
+                pltpu.make_async_copy(ig, ig_hbm, load_sem.at[0]).start()
+
+    def wg_copy(n):
+        columns = pl.ds(pl.multiple_of(n * col, col), col)
+        return pltpu.make_async_copy(wg_tile.at[n % 3], wg_hbm.at[:, columns], store_sem.at[n])
 
     def tiles(first, last):
         @pl.loop(first, last)
         def _(n):
+            @pl.when(n >= 3)
+            def _():
+                wg_copy(n - 3).wait()
+
             columns = pl.ds(pl.multiple_of(n * col, col), col)
-            wg_tile[:, columns] = jnp.dot(acts[...], hid[:, columns], preferred_element_type=jnp.float32)
-            pltpu.make_async_copy(wg_tile.at[:, columns], wg_hbm.at[:, columns], store_sem.at[n]).start()
-
-    act_step("own", 0)
+            wg_tile[n % 3] = jnp.dot(acts[...], hid[:, columns], preferred_element_type=jnp.float32)
+            wg_copy(n).start()
+
+    act_step(0)
     loads[3].wait()
     partial(0, yl)
-    y_send(0, yl)
-    act_other()
-    act_step("own", 1)
-
+    z_step(0, 1, yl)
+    act_step(1)
     for k in range(2):
         block = rows(x, other, c, k)
         arrived(("yl", k), block)
@@ -293,22 +333,28 @@
         arrived(("xm_own", k), rows(xat(1), yl, c, k))
     sibling(1)
     sibling(2)
-    act_step("other", 0)
-
     send(("xp_f",), rows(xat(-1), yl, c, 0), XP)
     send(("xm_f",), rows(xat(1), yl, c, 1), XM)
+    act_send(0)
+    act_send(1)
+    act_send(5)
+    act_send(2)
+    act_send(6)
+    z_step(0, 2, yl)
     partial(1, yl)
-    y_send(1, yl)
+    z_step(1, 1, yl)
     partial(2, yl)
-    y_send(2, yl)
+    z_step(2, 1, yl)
     partial(0, other)
-    y_send(0, other)
-    act_step("own", 2)
-    act_step("other", 1)
-
-    arrived(("xp_f",), rows(xat(2), yl, c, 0))
-    arrived(("xm_f",), rows(xat(2), yl, c, 1))
-    sibling(3)
+    z_step(0, 1, other)
+    act_step(2)
+    act_send(3)
+    act_send(7)
+    z_step(0, 3, yl)
+    z_step(1, 2, yl)
+    z_step(2, 2, yl)
+    act_step(3)
+    act_send(4)
     for k in range(2):
         arrived(("xp_yl", k), rows(xat(-1), other, c, k))
         arrived(("xm_yl", k), rows(xat(1), other, c, k))
@@ -318,64 +364,79 @@
             send(("xm_fy",), rows(xat(1), other, c, 1), XM)
     sibling(5)
     sibling(6)
+    partial(1, other)
+    z_step(1, 1, other)
+    partial(2, other)
+    z_step(2, 1, other)
+    z_step(0, 2, other)
+    z_step(0, 4, yl)
+    arrived(("xp_f",), rows(xat(2), yl, c, 0))
+    arrived(("xm_f",), rows(xat(2), yl, c, 1))
+    sibling(3)
     partial(3, yl)
-    y_send(3, yl)
-    act_step("own", 3)
-    act_step("other", 2)
-    partial(1, other)
-    y_send(1, other)
-    partial(2, other)
-    y_send(2, other)
-
-    act_step("other", 3)
-    z_step(0, 1)
-    z_step(0, 2)
-    z_step(1, 1)
-    z_step(2, 1)
-    z_step(0, 3)
+    z_step(3, 1, yl)
+    z_step(1, 3, yl)
+    z_step(2, 3, yl)
+    z_step(0, 3, other)
+    z_step(0, 5, yl)
+    z_step(1, 2, other)
+    z_step(2, 2, other)
     arrived(("xp_fy",), rows(xat(2), other, c, 0))
     arrived(("xm_fy",), rows(xat(2), other, c, 1))
     sibling(7)
-    z_step(1, 2)
-    z_step(2, 2)
-
     partial(3, other)
-    y_send(3, other)
-    z_step(0, 4)
-    z_step(1, 3)
-    z_step(2, 3)
-    tiles(0, 2)
-    z_step(0, 5)
-    z_step(1, 4)
-    z_step(2, 4)
-    tiles(2, 4)
-    z_step(3, 1)
-    tiles(4, 5)
-    z_step(3, 2)
-    tiles(5, 6)
-    z_step(1, 5)
-    z_step(2, 5)
-    z_step(3, 3)
-    tiles(6, 7)
-    z_step(3, 4)
-    tiles(7, n_cols)
-    z_step(3, 5)
+    z_step(3, 1, other)
+    z_step(3, 2, yl)
+    z_step(1, 4, yl)
+    z_step(2, 4, yl)
+    z_step(0, 4, other)
+    z_step(1, 3, other)
+    z_step(2, 3, other)
+    z_step(3, 3, yl)
+    z_step(3, 2, other)
+    acts_arrived()
+    z_step(1, 5, yl)
+    z_step(2, 5, yl)
+    z_step(0, 5, other)
+    tiles(0, 1)
+    z_step(1, 4, other)
+    z_step(2, 4, other)
+    z_step(3, 4, yl)
+    z_step(3, 3, other)
+    tiles(1, 3)
+    z_step(1, 5, other)
+    z_step(2, 5, other)
+    z_step(3, 5, yl)
+    z_step(3, 4, other)
+    tiles(3, 5)
+    z_step(3, 5, other)
+    tiles(5, 9)
+    finish(0)
+    finish(1)
+    finish(2)
+    finish(3)
 
     for copy in copies:
         copy.wait_send()
     for q in range(4):
         for b in range(2):
-            y_copy(q, b).wait_send()
             _, k = z_place(q, b)
+            if q not in Z_FIRST:
+                y_copy(q, b).wait_send()
+            else:
+                @pl.when(k == 0)
+                def _():
+                    y_copy(q, b).wait_send()
 
             @pl.when(k != 0)
             def _():
                 for h in range(2):
-                    z_copy(q, b, h).wait_send()
-
-    for n in range(n_cols):
-        columns = pl.ds(n * col, col)
-        pltpu.make_async_copy(wg_tile.at[:, columns], wg_hbm.at[:, columns], store_sem.at[n]).wait()
+                    z_copy(q, b, h, yh).wait_send()
+                    if q in Z_FIRST:
+                        z_copy(q, b, h, other_row).wait_send()
+
+    for n in range(n_cols - 3, n_cols):
+        wg_copy(n).wait()
     pltpu.make_async_copy(ig, ig_hbm, load_sem.at[0]).wait()
 
 
@@ -401,20 +462,21 @@
                 pltpu.VMEM((feats, hidden), bf16),
                 pltpu.VMEM((all_tokens, hidden), bf16),
                 pltpu.VMEM((feats, all_tokens), bf16),
-                pltpu.VMEM((NZ, tokens, feats), f32),
+                pltpu.VMEM((2 * NZ, tokens, feats), f32),
                 pltpu.VMEM((NZ, tokens, feats), bf16),
                 pltpu.VMEM((NZ, tokens, feats), bf16),
-                pltpu.VMEM((NZ, tokens, feats), bf16),
-                pltpu.VMEM((2, NZ, tokens, feats), bf16),
+                pltpu.VMEM((2 * NZ, tokens, feats), bf16),
+                pltpu.VMEM((2, 2 * NZ, tokens, feats), bf16),
+                pltpu.VMEM((tokens, feats), f32),
                 pltpu.VMEM((tokens, feats), bf16),
-                pltpu.VMEM((feats, hidden), f32),
+                pltpu.VMEM((3, feats, 256), f32),
                 pltpu.SemaphoreType.DMA((len(NAMES),)),
                 pltpu.SemaphoreType.DMA((len(NAMES),)),
                 pltpu.SemaphoreType.DMA((4,)),
                 pltpu.SemaphoreType.DMA((hidden // 256,)),
             ],
             compiler_params=pltpu.CompilerParams(
-                collective_id=0, has_side_effects=True, vmem_limit_bytes=42 * 2**20
+                collective_id=0, has_side_effects=True, vmem_limit_bytes=40 * 2**20
             ),
             cost_estimate=pl.CostEstimate(
                 flops=4 * all_tokens * feats * hidden, bytes_accessed=12 * 2**20,

time: 101 us -> 93 us (0.921)
  Pallas kernels: 95.9 us -> 88.6 us
    pallas_call x1, Pallas kernels: 95.9 us -> 88.6 us  [body(): pl.pallas_call(kernel, out_shape=(jax.ShapeDtypeStruct((tokens, feats), b...]
where the time goes in v3:
time: 93 us; the launch traced here: 92.9 us
  Pallas kernels  88.6 us (95%)
  local copies, waits for them, and re-layouts  3.64 us (4%)
    pallas_call x1, Pallas kernels, body(): pl.pallas_call(kernel, out_shape=(jax.ShapeDtypeStruct((tokens, feats), b...  88.6 us
    unnamed x2, local copies, waits for them, and re-layouts  3.64 us

profile of v3, /device:TPU:12, one launch (start us, length us, event | category | flops | bytes accessed | tf_op | source)
XLA Modules:
  0.0 92.9 jit_solution(15256175515204845336)
XLA Ops:
  0.6 88.6 %ffn_input_backward.1 = (bf16[128,768]{1,0:T(8,128)(2,1)S(1)}, f32[768,2304]{1,0:T(8,128)S(1)}) custom-call(bf16[128,768]{1,0:T(8,128)(2,1)} %inputs_hbm.1, bf16[128,2304]{1,0:T(8,128)(2,1)} %pre_hbm.1, bf16[128,2304]{1,0:T(8,128)(2,1)} %grad_hbm.1, bf16[768,2304]{1,0:T(8,128)(2,1)} %weight_hbm.1), custom_call_target="tpu_custom_call" | custom-call | flops 14495514624 | bytes 12582912 | tf_op jit(solution)/shard_map/ffn_input_backward/pallas_call | solution.py:450
  89.2 0.7 copy.8
  89.9 3.0 %copy.9 = f32[768,2304]{1,0:T(8,128)} copy(f32[768,2304]{1,0:T(8,128)S(1)} %get-tuple-element.5) | data formatting | bytes 14155776

commit v4 on v3

--- a/solution.py
+++ b/solution.py
@@ -395,22 +395,24 @@
     z_step(3, 3, yl)
     z_step(3, 2, other)
     acts_arrived()
+    tiles(0, 1)
     z_step(1, 5, yl)
     z_step(2, 5, yl)
     z_step(0, 5, other)
-    tiles(0, 1)
+    tiles(1, 2)
     z_step(1, 4, other)
     z_step(2, 4, other)
     z_step(3, 4, yl)
     z_step(3, 3, other)
-    tiles(1, 3)
+    tiles(2, 4)
     z_step(1, 5, other)
     z_step(2, 5, other)
     z_step(3, 5, yl)
+    tiles(4, 5)
     z_step(3, 4, other)
-    tiles(3, 5)
+    tiles(5, 8)
     z_step(3, 5, other)
-    tiles(5, 9)
+    tiles(8, 9)
     finish(0)
     finish(1)
     finish(2)

time: 93 us -> 93.3 us (level)
  no operation moved by 1% of the time
where the time goes in v4:
time: 93.3 us; the launch traced here: 93.2 us
  Pallas kernels  89 us (95%)
  local copies, waits for them, and re-layouts  3.64 us (4%)
    pallas_call x1, Pallas kernels, body(): pl.pallas_call(kernel, out_shape=(jax.ShapeDtypeStruct((tokens, feats), b...  89 us
    unnamed x2, local copies, waits for them, and re-layouts  3.64 us

profile of v4, /device:TPU:12, one launch (start us, length us, event | category | flops | bytes accessed | tf_op | source)
XLA Modules:
  0.0 93.2 jit_solution(18419104420529735494)
XLA Ops:
  0.6 89.0 %ffn_input_backward.1 = (bf16[128,768]{1,0:T(8,128)(2,1)S(1)}, f32[768,2304]{1,0:T(8,128)S(1)}) custom-call(bf16[128,768]{1,0:T(8,128)(2,1)} %inputs_hbm.1, bf16[128,2304]{1,0:T(8,128)(2,1)} %pre_hbm.1, bf16[128,2304]{1,0:T(8,128)(2,1)} %grad_hbm.1, bf16[768,2304]{1,0:T(8,128)(2,1)} %weight_hbm.1), custom_call_target="tpu_custom_call" | custom-call | flops 14495514624 | bytes 12582912 | tf_op jit(solution)/shard_map/ffn_input_backward/pallas_call | solution.py:452
  89.6 0.7 copy.8
  90.3 3.0 %copy.9 = f32[768,2304]{1,0:T(8,128)} copy(f32[768,2304]{1,0:T(8,128)S(1)} %get-tuple-element.5) | data formatting | bytes 14155776
